TPU v7x, 32 devices: a whole 2x2x4 slice. The times are simulated.
32 devices in a mesh: loop: 8 (over z, core), grp: 4 (over y, x).
Axes of the slice: x: 2, y: 2, z: 4, core: 2. Of those that a mesh axis runs over, the one named last changes fastest.
Arguments:
- node_feats: bfloat16 [512, 8192], P(None, ('loop', 'grp')), may hold values from -6 to 6
- tile_vals: bfloat16 [8, 8, 10, 128, 128], P('loop'), may hold values from -0.375 to 0.375
- tile_rows: int32 [8, 8, 10], P('loop'), may hold values from 0 to 7
- tile_cols: int32 [8, 8, 10], P('loop'), may hold values from 0 to 7
- tile_count: int32 [8, 8], P('loop'), may hold values from 0 to 10, as said below
- degree: int32 [8192], P('loop'), may hold values from 1 to 8
- w_self: bfloat16 [512, 512], replicated, may hold values from -0.25 to 0.25
- w_neigh: bfloat16 [512, 512], replicated, may hold values from -0.25 to 0.25
Outputs:
- node_out: bfloat16 [512, 8192], P(None, ('loop', 'grp'))
Inputs may be any that keep to these rules, and one draw needn't show every extreme that they name: Only the first tile_count[j, t] slots of a pair are tiles of the graph; later slots hold values that belong to no edge. Some pair uses all 10 slots in every draw.
All inputs are finite; a program needn't handle non-finite values.
Results may differ from a plain program's by a relative error of at most 0.0035.
Values may be sent and summed in bfloat16 or wider, within the bound.
A program may use at most 64 MiB of HBM per device.

v0:
```python
import jax
import jax.numpy as jnp
from jax import lax
from jax.sharding import PartitionSpec as P


def from_behind(shard, axis, by):
    size = lax.axis_size(axis)
    return lax.ppermute(shard, axis, [(i, (i + by) % size) for i in range(size)])


def tile_terms(sources, tiles, row_ids, col_ids, filled):
    channels = sources.shape[0]
    tile_edge = tiles.shape[-1]
    slot_count = tiles.shape[0]
    block_count = sources.shape[1] // tile_edge
    grouped = sources.reshape(channels, block_count, tile_edge)
    block_ids = lax.iota(jnp.int32, block_count)
    picker = (col_ids[:, None] == block_ids[None, :]).astype(jnp.bfloat16)
    chosen = jnp.einsum("kb,fbc->kfc", picker, grouped, preferred_element_type=jnp.float32).astype(
        jnp.bfloat16
    )
    products = jnp.einsum("kfc,krc->kfr", chosen, tiles, preferred_element_type=jnp.float32)
    active = lax.iota(jnp.int32, slot_count) < filled
    placer = ((row_ids[:, None] == block_ids[None, :]) & active[:, None]).astype(jnp.float32)
    spread = jnp.einsum(
        "kb,kfr->fbr",
        placer,
        products,
        precision=lax.Precision.HIGHEST,
        preferred_element_type=jnp.float32,
    )
    return spread.reshape(channels, block_count * tile_edge)


def project(weight, features):
    return lax.dot_general(
        weight, features, (((0,), (0,)), ((), ())), preferred_element_type=jnp.float32
    )


def shards(node_feats, tile_vals, tile_rows, tile_cols, tile_count, degree, w_self, w_neigh):
    cycle_size = lax.axis_size("loop")
    position = lax.axis_index("loop")
    columns = lax.all_to_all(node_feats, "grp", split_axis=0, concat_axis=1, tiled=True)
    own_tiles = tile_vals[0]
    own_rows = tile_rows[0]
    own_cols = tile_cols[0]
    own_counts = tile_count[0]

    def contribution(target):
        return tile_terms(
            columns,
            lax.dynamic_index_in_dim(own_tiles, target, 0, False),
            lax.dynamic_index_in_dim(own_rows, target, 0, False),
            lax.dynamic_index_in_dim(own_cols, target, 0, False),
            lax.dynamic_index_in_dim(own_counts, target, 0, False),
        )

    initial = contribution((position + 1) % cycle_size)

    def advance(offset, partial_value):
        arrived = from_behind(partial_value, "loop", -1)
        return arrived + contribution((position + offset + 1) % cycle_size)

    summed = lax.fori_loop(1, cycle_size, advance, initial)
    neighbor = (summed / degree.astype(jnp.float32)[None, :]).astype(jnp.bfloat16)
    node_major = lax.all_to_all(neighbor, "grp", split_axis=1, concat_axis=0, tiled=True)
    combined = project(w_self, node_feats) + project(w_neigh, node_major)
    hidden = jnp.maximum(combined, 0.0)
    mean_square = jnp.mean(hidden * hidden, axis=0, keepdims=True)
    return (hidden * lax.rsqrt(mean_square + 1e-05)).astype(jnp.bfloat16)


def solution(mesh):
    return jax.shard_map(
        shards,
        mesh=mesh,
        in_specs=(
            P(None, ("loop", "grp")),
            P("loop", None, None, None, None),
            P("loop", None, None),
            P("loop", None, None),
            P("loop", None),
            P("loop"),
            P(),
            P(),
        ),
        out_specs=P(None, ("loop", "grp")),
        check_vma=False,
    )
```

profile of v0, /device:TPU:0, one launch (start us, length us, event | category | flops | bytes accessed | tf_op | source)
XLA Modules:
  0.0 97.4 jit_solution(1738609470399780319)
XLA Ops:
  0.0 5.3 %all-to-all-start = ((bf16[4,128,256]{2,1,0:T(8,128)(2,1)}), bf16[4,128,256]{2,1,0:T(8,128)(2,1)S(1)}, u32[]{:S(2)}, u32[]{:S(2)}) async-start(bf16[4,128,256]{2,1,0:T(8,128)(2,1)} %bitcast.90), calls=%async_computation | async-start | bytes 524288 | tf_op jit(solution)/shard_map/all_to_all | solution.py:45
  6.0 1.3 %constant_dynamic-slice_fusion.2 = s32[1,1]{1,0:T(1,128)} fusion(s32[1,8]{1,0:T(1,128)} %param.14, s32[]{:T(128)S(6)} %select_n.47), kind=kLoop, calls=%fused_computation.45 | loop fusion | bytes 12 | tf_op jit(solution)/shard_map/jit(dynamic_index_in_dim)/dynamic_slice | solution.py:57
  8.6 2.0 %all-to-all-done = bf16[4,128,256]{2,1,0:T(8,128)(2,1)S(1)} async-done(((bf16[4,128,256]{2,1,0:T(8,128)(2,1)}), bf16[4,128,256]{2,1,0:T(8,128)(2,1)S(1)}, u32[]{:S(2)}, u32[]{:S(2)}) %all-to-all-start) | async-done | bytes 262176 | tf_op jit(solution)/shard_map/all_to_all | solution.py:45
  11.4 1.3 %fusion.21 = f32[10,128,128]{2,1,0:T(8,128)S(1)} fusion(bf16[10,128,128]{2,0,1:T(8,128)(2,1)S(1)} %convolution_convert_fusion.1, bf16[1,8,10,128,128]{4,3,2,1,0:T(8,128)(2,1)} %param.11, s32[]{:T(128)S(6)} %select_n.47), kind=kOutput, calls=%fused_computation.32 | convolution fusion | flops 41943040 | bytes 1310724 | tf_op jit(solution)/shard_map/kfc,krc->kfr/dot_general | solution.py:23
  12.7 1.0 %fusion.19 = f32[128,128,8]{1,2,0:T(8,128)S(1)} fusion(f32[10,128,128]{2,1,0:T(8,128)S(1)} %fusion.21, s32[10]{0:T(128)S(1)} %get-tuple-element.234, pred[10]{0:T(512)(128)(4,1)S(1)} %iota_compare_fusion.5), kind=kOutput, calls=%fused_computation.26 | convolution fusion | flops 15728800 | bytes 1179698 | tf_op jit(solution)/shard_map/kb,kfr->fbr/dot_general | solution.py:26
  14.1 72.1 %while.15 = (s32[]{:T(128)}, f32[128,1024]{1,0:T(8,128)S(1)}, s32[]{:T(128)}, s32[8,10]{1,0:T(8,128)}, bf16[128,1024]{1,0:T(8,128)(2,1)S(1)}, /*index=5*/bf16[8,...) while((s32[]{:T(128)}, f32[128,1024]{1,0:T(8,128)S(1)}, ...), condition=%wide.region_1.2_spmd, body=%wide.region_0.1_spmd.sunk | while | flops 60588296 | bytes 7275104 | solution.py:66
  14.1 1.7 %collective-permute-start = (f32[128,1024]{1,0:T(8,128)S(1)}, f32[128,1024]{1,0:T(8,128)S(1)}, u32[]{:S(2)}, u32[]{:S(2)}) collective-permute-start(f32[128,1024]{1,0:T(8,128)S(1)} %get-tuple-element.301), channel_id=1, source_target_pairs={{0,28},{4,0},{8,4},{12,8},{16,12},{20,16},{24,20},{28,24},{1,29},{... | collective-permute-start | bytes 1572872 | tf_op jit(solution)/shard_map/while/body/eval_jaxpr/ppermute | solution.py:9
  18.2 1.3 %fusion.59 = f32[10,128,128]{2,1,0:T(8,128)S(1)} fusion(bf16[10,128,128]{2,0,1:T(8,128)(2,1)S(1)} %convolution_convert_fusion.3, bf16[8,10,128,128]{3,2,1,0:T(8,128)(2,1)} %get-tuple-element.317, s32[]{:T(128)S(6)} %select_n.51), kind=kOutput, calls=%fused_computation.4.clone.1 | convolution fusion | flops 41943040 | bytes 1310724 | tf_op jit(solution)/shard_map/while/body/eval_jaxpr/kfc,krc->kfr/dot_general | solution.py:23
  19.6 1.0 %fusion.60 = f32[128,128,8]{1,2,0:T(8,128)S(1)} fusion(f32[10,128,128]{2,1,0:T(8,128)S(1)} %fusion.59, s32[10]{0:T(128)S(1)} %get-tuple-element.287, pred[10]{0:T(512)(128)(4,1)S(1)} %iota_compare_fusion.7), kind=kOutput, calls=%fused_computation.1.clone.1 | convolution fusion | flops 15728800 | bytes 1179698 | tf_op jit(solution)/shard_map/while/body/eval_jaxpr/kb,kfr->fbr/dot_general | solution.py:26
  20.5 2.0 %collective-permute-done = f32[128,1024]{1,0:T(8,128)S(1)} collective-permute-done((f32[128,1024]{1,0:T(8,128)S(1)}, f32[128,1024]{1,0:T(8,128)S(1)}, u32[]{:S(2)}, u32[]{:S(2)}) %collective-permute-start) | collective-permute-done | bytes 524320 | tf_op jit(solution)/shard_map/while/body/eval_jaxpr/ppermute | solution.py:9
  22.7 3.8 %collective-permute-start = (f32[128,1024]{1,0:T(8,128)S(1)}, f32[128,1024]{1,0:T(8,128)S(1)}, u32[]{:S(2)}, u32[]{:S(2)}) collective-permute-start(f32[128,1024]{1,0:T(8,128)S(1)} %get-tuple-element.301), channel_id=1, source_target_pairs={{0,28},{4,0},{8,4},{12,8},{16,12},{20,16},{24,20},{28,24},{1,29},{... | collective-permute-start | bytes 1572872 | tf_op jit(solution)/shard_map/while/body/eval_jaxpr/ppermute | solution.py:9
  28.8 1.3 %fusion.59 = f32[10,128,128]{2,1,0:T(8,128)S(1)} fusion(bf16[10,128,128]{2,0,1:T(8,128)(2,1)S(1)} %convolution_convert_fusion.3, bf16[8,10,128,128]{3,2,1,0:T(8,128)(2,1)} %get-tuple-element.317, s32[]{:T(128)S(6)} %select_n.51), kind=kOutput, calls=%fused_computation.4.clone.1 | convolution fusion | flops 41943040 | bytes 1310724 | tf_op jit(solution)/shard_map/while/body/eval_jaxpr/kfc,krc->kfr/dot_general | solution.py:23
  30.2 1.0 %fusion.60 = f32[128,128,8]{1,2,0:T(8,128)S(1)} fusion(f32[10,128,128]{2,1,0:T(8,128)S(1)} %fusion.59, s32[10]{0:T(128)S(1)} %get-tuple-element.287, pred[10]{0:T(512)(128)(4,1)S(1)} %iota_compare_fusion.7), kind=kOutput, calls=%fused_computation.1.clone.1 | convolution fusion | flops 15728800 | bytes 1179698 | tf_op jit(solution)/shard_map/while/body/eval_jaxpr/kb,kfr->fbr/dot_general | solution.py:26
  31.1 2.0 %collective-permute-done = f32[128,1024]{1,0:T(8,128)S(1)} collective-permute-done((f32[128,1024]{1,0:T(8,128)S(1)}, f32[128,1024]{1,0:T(8,128)S(1)}, u32[]{:S(2)}, u32[]{:S(2)}) %collective-permute-start) | collective-permute-done | bytes 524320 | tf_op jit(solution)/shard_map/while/body/eval_jaxpr/ppermute | solution.py:9
  33.3 3.8 %collective-permute-start = (f32[128,1024]{1,0:T(8,128)S(1)}, f32[128,1024]{1,0:T(8,128)S(1)}, u32[]{:S(2)}, u32[]{:S(2)}) collective-permute-start(f32[128,1024]{1,0:T(8,128)S(1)} %get-tuple-element.301), channel_id=1, source_target_pairs={{0,28},{4,0},{8,4},{12,8},{16,12},{20,16},{24,20},{28,24},{1,29},{... | collective-permute-start | bytes 1572872 | tf_op jit(solution)/shard_map/while/body/eval_jaxpr/ppermute | solution.py:9
  39.4 1.3 %fusion.59 = f32[10,128,128]{2,1,0:T(8,128)S(1)} fusion(bf16[10,128,128]{2,0,1:T(8,128)(2,1)S(1)} %convolution_convert_fusion.3, bf16[8,10,128,128]{3,2,1,0:T(8,128)(2,1)} %get-tuple-element.317, s32[]{:T(128)S(6)} %select_n.51), kind=kOutput, calls=%fused_computation.4.clone.1 | convolution fusion | flops 41943040 | bytes 1310724 | tf_op jit(solution)/shard_map/while/body/eval_jaxpr/kfc,krc->kfr/dot_general | solution.py:23
  40.8 1.0 %fusion.60 = f32[128,128,8]{1,2,0:T(8,128)S(1)} fusion(f32[10,128,128]{2,1,0:T(8,128)S(1)} %fusion.59, s32[10]{0:T(128)S(1)} %get-tuple-element.287, pred[10]{0:T(512)(128)(4,1)S(1)} %iota_compare_fusion.7), kind=kOutput, calls=%fused_computation.1.clone.1 | convolution fusion | flops 15728800 | bytes 1179698 | tf_op jit(solution)/shard_map/while/body/eval_jaxpr/kb,kfr->fbr/dot_general | solution.py:26
  41.7 2.0 %collective-permute-done = f32[128,1024]{1,0:T(8,128)S(1)} collective-permute-done((f32[128,1024]{1,0:T(8,128)S(1)}, f32[128,1024]{1,0:T(8,128)S(1)}, u32[]{:S(2)}, u32[]{:S(2)}) %collective-permute-start) | collective-permute-done | bytes 524320 | tf_op jit(solution)/shard_map/while/body/eval_jaxpr/ppermute | solution.py:9
  43.9 3.8 %collective-permute-start = (f32[128,1024]{1,0:T(8,128)S(1)}, f32[128,1024]{1,0:T(8,128)S(1)}, u32[]{:S(2)}, u32[]{:S(2)}) collective-permute-start(f32[128,1024]{1,0:T(8,128)S(1)} %get-tuple-element.301), channel_id=1, source_target_pairs={{0,28},{4,0},{8,4},{12,8},{16,12},{20,16},{24,20},{28,24},{1,29},{... | collective-permute-start | bytes 1572872 | tf_op jit(solution)/shard_map/while/body/eval_jaxpr/ppermute | solution.py:9
  50.0 1.3 %fusion.59 = f32[10,128,128]{2,1,0:T(8,128)S(1)} fusion(bf16[10,128,128]{2,0,1:T(8,128)(2,1)S(1)} %convolution_convert_fusion.3, bf16[8,10,128,128]{3,2,1,0:T(8,128)(2,1)} %get-tuple-element.317, s32[]{:T(128)S(6)} %select_n.51), kind=kOutput, calls=%fused_computation.4.clone.1 | convolution fusion | flops 41943040 | bytes 1310724 | tf_op jit(solution)/shard_map/while/body/eval_jaxpr/kfc,krc->kfr/dot_general | solution.py:23
  52.3 2.0 %collective-permute-done = f32[128,1024]{1,0:T(8,128)S(1)} collective-permute-done((f32[128,1024]{1,0:T(8,128)S(1)}, f32[128,1024]{1,0:T(8,128)S(1)}, u32[]{:S(2)}, u32[]{:S(2)}) %collective-permute-start) | collective-permute-done | bytes 524320 | tf_op jit(solution)/shard_map/while/body/eval_jaxpr/ppermute | solution.py:9
  54.5 3.8 %collective-permute-start = (f32[128,1024]{1,0:T(8,128)S(1)}, f32[128,1024]{1,0:T(8,128)S(1)}, u32[]{:S(2)}, u32[]{:S(2)}) collective-permute-start(f32[128,1024]{1,0:T(8,128)S(1)} %get-tuple-element.301), channel_id=1, source_target_pairs={{0,28},{4,0},{8,4},{12,8},{16,12},{20,16},{24,20},{28,24},{1,29},{... | collective-permute-start | bytes 1572872 | tf_op jit(solution)/shard_map/while/body/eval_jaxpr/ppermute | solution.py:9
  60.6 1.3 %fusion.59 = f32[10,128,128]{2,1,0:T(8,128)S(1)} fusion(bf16[10,128,128]{2,0,1:T(8,128)(2,1)S(1)} %convolution_convert_fusion.3, bf16[8,10,128,128]{3,2,1,0:T(8,128)(2,1)} %get-tuple-element.317, s32[]{:T(128)S(6)} %select_n.51), kind=kOutput, calls=%fused_computation.4.clone.1 | convolution fusion | flops 41943040 | bytes 1310724 | tf_op jit(solution)/shard_map/while/body/eval_jaxpr/kfc,krc->kfr/dot_general | solution.py:23
  62.9 2.0 %collective-permute-done = f32[128,1024]{1,0:T(8,128)S(1)} collective-permute-done((f32[128,1024]{1,0:T(8,128)S(1)}, f32[128,1024]{1,0:T(8,128)S(1)}, u32[]{:S(2)}, u32[]{:S(2)}) %collective-permute-start) | collective-permute-done | bytes 524320 | tf_op jit(solution)/shard_map/while/body/eval_jaxpr/ppermute | solution.py:9
  65.1 3.8 %collective-permute-start = (f32[128,1024]{1,0:T(8,128)S(1)}, f32[128,1024]{1,0:T(8,128)S(1)}, u32[]{:S(2)}, u32[]{:S(2)}) collective-permute-start(f32[128,1024]{1,0:T(8,128)S(1)} %get-tuple-element.301), channel_id=1, source_target_pairs={{0,28},{4,0},{8,4},{12,8},{16,12},{20,16},{24,20},{28,24},{1,29},{... | collective-permute-start | bytes 1572872 | tf_op jit(solution)/shard_map/while/body/eval_jaxpr/ppermute | solution.py:9
  71.2 1.3 %fusion.59 = f32[10,128,128]{2,1,0:T(8,128)S(1)} fusion(bf16[10,128,128]{2,0,1:T(8,128)(2,1)S(1)} %convolution_convert_fusion.3, bf16[8,10,128,128]{3,2,1,0:T(8,128)(2,1)} %get-tuple-element.317, s32[]{:T(128)S(6)} %select_n.51), kind=kOutput, calls=%fused_computation.4.clone.1 | convolution fusion | flops 41943040 | bytes 1310724 | tf_op jit(solution)/shard_map/while/body/eval_jaxpr/kfc,krc->kfr/dot_general | solution.py:23
  73.5 2.0 %collective-permute-done = f32[128,1024]{1,0:T(8,128)S(1)} collective-permute-done((f32[128,1024]{1,0:T(8,128)S(1)}, f32[128,1024]{1,0:T(8,128)S(1)}, u32[]{:S(2)}, u32[]{:S(2)}) %collective-permute-start) | collective-permute-done | bytes 524320 | tf_op jit(solution)/shard_map/while/body/eval_jaxpr/ppermute | solution.py:9
  75.7 3.8 %collective-permute-start = (f32[128,1024]{1,0:T(8,128)S(1)}, f32[128,1024]{1,0:T(8,128)S(1)}, u32[]{:S(2)}, u32[]{:S(2)}) collective-permute-start(f32[128,1024]{1,0:T(8,128)S(1)} %get-tuple-element.301), channel_id=1, source_target_pairs={{0,28},{4,0},{8,4},{12,8},{16,12},{20,16},{24,20},{28,24},{1,29},{... | collective-permute-start | bytes 1572872 | tf_op jit(solution)/shard_map/while/body/eval_jaxpr/ppermute | solution.py:9
  81.8 1.3 %fusion.59 = f32[10,128,128]{2,1,0:T(8,128)S(1)} fusion(bf16[10,128,128]{2,0,1:T(8,128)(2,1)S(1)} %convolution_convert_fusion.3, bf16[8,10,128,128]{3,2,1,0:T(8,128)(2,1)} %get-tuple-element.317, s32[]{:T(128)S(6)} %select_n.51), kind=kOutput, calls=%fused_computation.4.clone.1 | convolution fusion | flops 41943040 | bytes 1310724 | tf_op jit(solution)/shard_map/while/body/eval_jaxpr/kfc,krc->kfr/dot_general | solution.py:23
  84.1 2.0 %collective-permute-done = f32[128,1024]{1,0:T(8,128)S(1)} collective-permute-done((f32[128,1024]{1,0:T(8,128)S(1)}, f32[128,1024]{1,0:T(8,128)S(1)}, u32[]{:S(2)}, u32[]{:S(2)}) %collective-permute-start) | collective-permute-done | bytes 524320 | tf_op jit(solution)/shard_map/while/body/eval_jaxpr/ppermute | solution.py:9
  87.4 3.4 %all-to-all-start.1 = ((bf16[128,4,256]{0,2,1:T(8,128)(2,1)}), bf16[128,4,256]{0,2,1:T(8,128)(2,1)S(1)}, u32[]{:S(2)}, u32[]{:S(2)}) async-start(bf16[128,4,256]{0,2,1:T(8,128)(2,1)} %bitcast.22), calls=%async_computation.1 | async-start | bytes 524288 | tf_op jit(solution)/shard_map/all_to_all | solution.py:68
  91.1 5.0 %all-to-all-done.1 = bf16[128,4,256]{0,2,1:T(8,128)(2,1)S(1)} async-done(((bf16[128,4,256]{0,2,1:T(8,128)(2,1)}), bf16[128,4,256]{0,2,1:T(8,128)(2,1)S(1)}, u32[]{:S(2)}, u32[]{:S(2)}) %all-to-all-start.1) | async-done | bytes 262176 | tf_op jit(solution)/shard_map/all_to_all | solution.py:68
  (70 shorter events, 27.2 us)
Async XLA Ops:
  0.0 96.3 %copy-start = (bf16[512,512]{1,0:T(8,128)(2,1)S(1)}, bf16[512,512]{1,0:T(8,128)(2,1)}, u32[]{:S(2)}) copy-start(bf16[512,512]{1,0:T(8,128)(2,1)} %param.17) | copy-start | bytes 1572868
  0.0 10.7 %all-to-all-start = ((bf16[4,128,256]{2,1,0:T(8,128)(2,1)}), bf16[4,128,256]{2,1,0:T(8,128)(2,1)S(1)}, u32[]{:S(2)}, u32[]{:S(2)}) async-start(bf16[4,128,256]{2,1,0:T(8,128)(2,1)} %bitcast.90), calls=%async_computation | async-start | bytes 524288 | tf_op jit(solution)/shard_map/all_to_all | solution.py:45
  11.3 2.8 %copy-start.3 = (s32[1,8]{1,0:T(1,128)S(1)}, s32[1,8]{1,0:T(1,128)}, u32[]{:S(2)}) copy-start(s32[1,8]{1,0:T(1,128)} %param.14) | copy-start | bytes 100
  14.1 76.7 %copy-start.1 = (bf16[512,256]{1,0:T(8,128)(2,1)S(1)}, bf16[512,256]{1,0:T(8,128)(2,1)}, u32[]{:S(2)}) copy-start(bf16[512,256]{1,0:T(8,128)(2,1)} %param.10) | copy-start | bytes 786436
  14.1 76.7 %copy-start.2 = (bf16[512,512]{1,0:T(8,128)(2,1)S(1)}, bf16[512,512]{1,0:T(8,128)(2,1)}, u32[]{:S(2)}) copy-start(bf16[512,512]{1,0:T(8,128)(2,1)} %param.16) | copy-start | bytes 1572868
  14.1 8.4 %collective-permute-start = (f32[128,1024]{1,0:T(8,128)S(1)}, f32[128,1024]{1,0:T(8,128)S(1)}, u32[]{:S(2)}, u32[]{:S(2)}) collective-permute-start(f32[128,1024]{1,0:T(8,128)S(1)} %get-tuple-element.301), channel_id=1, source_target_pairs={{0,28},{4,0},{8,4},{12,8},{16,12},{20,16},{24,20},{28,24},{1,29},{... | collective-permute-start | bytes 1572872 | tf_op jit(solution)/shard_map/while/body/eval_jaxpr/ppermute | solution.py:9
  22.7 10.5 %collective-permute-start = (f32[128,1024]{1,0:T(8,128)S(1)}, f32[128,1024]{1,0:T(8,128)S(1)}, u32[]{:S(2)}, u32[]{:S(2)}) collective-permute-start(f32[128,1024]{1,0:T(8,128)S(1)} %get-tuple-element.301), channel_id=1, source_target_pairs={{0,28},{4,0},{8,4},{12,8},{16,12},{20,16},{24,20},{28,24},{1,29},{... | collective-permute-start | bytes 1572872 | tf_op jit(solution)/shard_map/while/body/eval_jaxpr/ppermute | solution.py:9
  33.3 10.5 %collective-permute-start = (f32[128,1024]{1,0:T(8,128)S(1)}, f32[128,1024]{1,0:T(8,128)S(1)}, u32[]{:S(2)}, u32[]{:S(2)}) collective-permute-start(f32[128,1024]{1,0:T(8,128)S(1)} %get-tuple-element.301), channel_id=1, source_target_pairs={{0,28},{4,0},{8,4},{12,8},{16,12},{20,16},{24,20},{28,24},{1,29},{... | collective-permute-start | bytes 1572872 | tf_op jit(solution)/shard_map/while/body/eval_jaxpr/ppermute | solution.py:9
  43.9 10.5 %collective-permute-start = (f32[128,1024]{1,0:T(8,128)S(1)}, f32[128,1024]{1,0:T(8,128)S(1)}, u32[]{:S(2)}, u32[]{:S(2)}) collective-permute-start(f32[128,1024]{1,0:T(8,128)S(1)} %get-tuple-element.301), channel_id=1, source_target_pairs={{0,28},{4,0},{8,4},{12,8},{16,12},{20,16},{24,20},{28,24},{1,29},{... | collective-permute-start | bytes 1572872 | tf_op jit(solution)/shard_map/while/body/eval_jaxpr/ppermute | solution.py:9
  54.5 10.5 %collective-permute-start = (f32[128,1024]{1,0:T(8,128)S(1)}, f32[128,1024]{1,0:T(8,128)S(1)}, u32[]{:S(2)}, u32[]{:S(2)}) collective-permute-start(f32[128,1024]{1,0:T(8,128)S(1)} %get-tuple-element.301), channel_id=1, source_target_pairs={{0,28},{4,0},{8,4},{12,8},{16,12},{20,16},{24,20},{28,24},{1,29},{... | collective-permute-start | bytes 1572872 | tf_op jit(solution)/shard_map/while/body/eval_jaxpr/ppermute | solution.py:9
  65.1 10.5 %collective-permute-start = (f32[128,1024]{1,0:T(8,128)S(1)}, f32[128,1024]{1,0:T(8,128)S(1)}, u32[]{:S(2)}, u32[]{:S(2)}) collective-permute-start(f32[128,1024]{1,0:T(8,128)S(1)} %get-tuple-element.301), channel_id=1, source_target_pairs={{0,28},{4,0},{8,4},{12,8},{16,12},{20,16},{24,20},{28,24},{1,29},{... | collective-permute-start | bytes 1572872 | tf_op jit(solution)/shard_map/while/body/eval_jaxpr/ppermute | solution.py:9
  75.7 10.5 %collective-permute-start = (f32[128,1024]{1,0:T(8,128)S(1)}, f32[128,1024]{1,0:T(8,128)S(1)}, u32[]{:S(2)}, u32[]{:S(2)}) collective-permute-start(f32[128,1024]{1,0:T(8,128)S(1)} %get-tuple-element.301), channel_id=1, source_target_pairs={{0,28},{4,0},{8,4},{12,8},{16,12},{20,16},{24,20},{28,24},{1,29},{... | collective-permute-start | bytes 1572872 | tf_op jit(solution)/shard_map/while/body/eval_jaxpr/ppermute | solution.py:9
  87.4 8.8 %all-to-all-start.1 = ((bf16[128,4,256]{0,2,1:T(8,128)(2,1)}), bf16[128,4,256]{0,2,1:T(8,128)(2,1)S(1)}, u32[]{:S(2)}, u32[]{:S(2)}) async-start(bf16[128,4,256]{0,2,1:T(8,128)(2,1)} %bitcast.22), calls=%async_computation.1 | async-start | bytes 524288 | tf_op jit(solution)/shard_map/all_to_all | solution.py:68
where the time goes:
time: 98.3 us; the launch traced here: 97.4 us
  starting transfers between devices  32.9 us (33%)
  matrix products  21.9 us (22%)
  waiting for transfers between devices  20.9 us (21%)
  local copies, waits for them, and re-layouts  12.9 us (13%)
  other arithmetic  8.25 us (8%)
    ppermute x7, starting transfers between devices, from_behind(): lax.ppermute(shard, axis, [(i, (i + by) % size) for i in range(size)])  24.2 us
    ppermute x7, waiting for transfers between devices, from_behind(): lax.ppermute(shard, axis, [(i, (i + by) % size) for i in range(size)])  13.9 us
    dot_general x8, matrix products, tile_terms(): jnp.einsum('kfc,krc->kfr', chosen, tiles, preferred_element_type=jnp.floa...  10.6 us
    dot_general x8, matrix products, tile_terms(): jnp.einsum('kb,kfr->fbr', placer, products, precision=lax.Precision.HIGHE...  7.83 us
    dynamic_slice x8, local copies, waits for them, and re-layouts, contribution(): lax.dynamic_index_in_dim(own_counts, target, 0, False)  5.85 us
    eq x8, local copies, waits for them, and re-layouts, tile_terms(): picker = (col_ids[:, None] == block_ids[None, :]).astype(jnp.bfloat16)  5.67 us
    all_to_all x1, starting transfers between devices, shards(): lax.all_to_all(node_feats, 'grp', split_axis=0, concat_axis=1, tiled=True)  5.29 us
    lt x8, other arithmetic, tile_terms(): active = lax.iota(jnp.int32, slot_count) < filled  5 us
  transfers between devices with their start and end apart: 9, of which 9 were waited for; matrix products, arithmetic and copies ran while one was open for 37% of the time, Pallas kernels for 0%

commit v1 on v0

v1 whole, which is shorter than its diff:
```python
import functools

import jax
import jax.numpy as jnp
from jax import lax
from jax.experimental import pallas as pl
from jax.experimental.pallas import tpu as pltpu
from jax.sharding import PartitionSpec as P

MESH = pl.DeviceIdType.MESH
CHUNKS = 4


def kernel(
    chips, groups, chunks,
    feats, tiles_hbm, w_self_hbm, w_neigh_hbm, rows, cols, counts, degree,
    out,
    *scratch,
):
    columns = scratch[:chunks]
    (
        tiles, w_self, w_neigh, w_neigh_t, pre, own, mate_out, mate_in, chain_out, from_low, from_high,
        local_sem, own_sem, gather_send, gather_recv, mate_send, mate_recv,
        chain_send, low_recv, high_recv,
    ) = scratch[chunks:]
    position = lax.axis_index("loop")
    g = lax.axis_index("grp")
    z, core = position // 2, position % 2
    features, nodes = feats.shape
    part = features // chunks
    slots, edge = tiles.shape[1], tiles.shape[2]
    per = nodes // edge

    copies = [
        pltpu.make_async_copy(tiles_hbm, tiles, local_sem.at[0]),
        pltpu.make_async_copy(w_self_hbm, w_self, local_sem.at[1]),
        pltpu.make_async_copy(w_neigh_hbm, w_neigh, local_sem.at[2]),
    ]

    def own_copy(q, r):
        return pltpu.make_async_copy(
            feats.at[pl.ds(q * part, part), pl.ds(r * edge, edge)],
            columns[q].at[g * per + r],
            own_sem.at[q, r],
        )

    def gather(q, offset, r):
        return pltpu.make_async_remote_copy(
            src_ref=feats.at[pl.ds(q * part, part), pl.ds(r * edge, edge)],
            dst_ref=columns[q].at[g * per + r],
            send_sem=gather_send.at[q, offset - 1, r],
            recv_sem=gather_recv.at[q, offset - 1, r],
            device_id={"grp": lax.rem(g + offset, groups)},
            device_id_type=MESH,
        )

    def mate_copy(q, zt):
        return pltpu.make_async_remote_copy(
            src_ref=mate_out.at[zt, q],
            dst_ref=mate_in.at[zt, q],
            send_sem=mate_send.at[zt, q],
            recv_sem=mate_recv.at[zt, q],
            device_id={"loop": z * 2 + 1 - core},
            device_id_type=MESH,
        )

    def up_copy(q, zt):
        return pltpu.make_async_remote_copy(
            src_ref=chain_out.at[zt, q],
            dst_ref=from_low.at[zt, q],
            send_sem=chain_send.at[zt, q],
            recv_sem=low_recv.at[zt, q],
            device_id={"loop": position + 2},
            device_id_type=MESH,
        )

    def down_copy(q, zt):
        return pltpu.make_async_remote_copy(
            src_ref=chain_out.at[zt, q],
            dst_ref=from_high.at[zt, q],
            send_sem=chain_send.at[zt, q],
            recv_sem=high_recv.at[zt, q],
            device_id={"loop": position - 2},
            device_id_type=MESH,
        )

    for q in range(chunks):
        for r in range(per):
            own_copy(q, r).start()
    for copy in copies:
        copy.start()

    barrier = pltpu.get_barrier_semaphore()
    for offset in range(1, groups):
        pl.semaphore_signal(
            barrier, inc=1, device_id={"grp": lax.rem(g + offset, groups)}, device_id_type=MESH
        )
    pl.semaphore_signal(
        barrier, inc=1, device_id={"loop": z * 2 + 1 - core}, device_id_type=MESH
    )

    @pl.when(z > 0)
    def _():
        pl.semaphore_signal(
            barrier, inc=1, device_id={"loop": position - 2}, device_id_type=MESH
        )

    @pl.when(z < chips - 1)
    def _():
        pl.semaphore_signal(
            barrier, inc=1, device_id={"loop": position + 2}, device_id_type=MESH
        )

    inner = jnp.where((z > 0) & (z < chips - 1), 1, 0)
    pl.semaphore_wait(barrier, groups + 1 + inner)

    for q in range(chunks):
        for offset in range(1, groups):
            for r in range(per):
                gather(q, offset, r).start()

    def masked(t, k):
        tile = tiles[t, k]
        block = rows[t, k] - g * per
        live = (k < counts[0, t]).astype(jnp.int32)
        return jnp.concatenate(
            [
                tile * ((block == r).astype(jnp.int32) * live).astype(jnp.float32).astype(tile.dtype)
                for r in range(per)
            ],
            axis=0,
        )

    def picked(q, t, k):
        return columns[q][cols[t, k]]

    def partial(q, t):
        total = None
        for k in range(0, slots, 2):
            pair = range(k, min(k + 2, slots))
            left = jnp.concatenate([picked(q, t, s) for s in pair], axis=1)
            right = jnp.concatenate([masked(t, s) for s in pair], axis=1)
            term = lax.dot_general(
                left, right, (((1,), (1,)), ((), ())), preferred_element_type=jnp.float32
            )
            total = term if total is None else total + term
        return total

    upward = 2 * z < chips

    def target_at(i):
        return jnp.where(upward, chips - 1 - i, i)

    def mate_step(q, i):
        zt = target_at(i)
        mate_out[zt, q] = partial(q, zt * 2 + 1 - core)
        mate_copy(q, zt).start()

    def compute(q):
        for offset in range(1, groups):
            for r in range(per):
                gather(q, offset, r).wait_recv()
        if q == 0:
            for r in range(per):
                own_copy(q, r).wait()
            copies[0].wait()
        mate_step(q, 0)

        @pl.loop(0, chips)
        def _(i):
            @pl.when(i + 1 < chips)
            def _():
                mate_step(q, i + 1)

            zt = target_at(i)
            mine = partial(q, zt * 2 + core)
            mate_copy(q, zt).wait_recv()
            mine = mine + mate_in[zt, q]
            own[zt, q] = mine

            @pl.when((z == 0) & (zt > 0))
            def _():
                chain_out[zt, q] = mine.astype(chain_out.dtype)
                up_copy(q, zt).start()

            @pl.when((z == chips - 1) & (zt < chips - 1))
            def _():
                chain_out[zt, q] = mine.astype(chain_out.dtype)
                down_copy(q, zt).start()

    def relay(q):
        @pl.loop(0, chips - 1)
        def _(d):
            high = chips - 1 - d

            @pl.when((z > 0) & (high > z))
            def _():
                up_copy(q, high).wait_recv()
                chain_out[high, q] = (
                    own[high, q] + from_low[high, q].astype(jnp.float32)
                ).astype(chain_out.dtype)
                up_copy(q, high).start()

            @pl.when((z < chips - 1) & (d < z))
            def _():
                down_copy(q, d).wait_recv()
                chain_out[d, q] = (
                    own[d, q] + from_high[d, q].astype(jnp.float32)
                ).astype(chain_out.dtype)
                down_copy(q, d).start()

        @pl.when(z > 0)
        def _():
            up_copy(q, z).wait_recv()
            own[z, q] += from_low[z, q].astype(jnp.float32)

        @pl.when(z < chips - 1)
        def _():
            down_copy(q, z).wait_recv()
            own[z, q] += from_high[z, q].astype(jnp.float32)

        start = pl.multiple_of(g * nodes, nodes)
        norm = degree[:, pl.ds(start, nodes)].astype(jnp.float32)
        neighbor = (own[z, q] / norm).astype(jnp.bfloat16)
        pre[...] += jnp.dot(
            w_neigh_t[:, q * part:(q + 1) * part], neighbor, preferred_element_type=jnp.float32
        )

    for q in range(chunks):
        compute(q)
        if q == 0:
            copies[1].wait()
            copies[2].wait()
            for later in range(1, chunks):
                for r in range(per):
                    own_copy(later, r).wait()
            w_neigh_t[...] = w_neigh[...].T
            total = None
            for piece in range(chunks):
                term = lax.dot_general(
                    w_self[piece * part:(piece + 1) * part, :],
                    jnp.concatenate([columns[piece][g * per + r] for r in range(per)], axis=1),
                    (((0,), (0,)), ((), ())),
                    preferred_element_type=jnp.float32,
                )
                total = term if total is None else total + term
            pre[...] = total
        else:
            relay(q - 1)
    relay(chunks - 1)

    hidden = jnp.maximum(pre[...], 0.0)
    mean_square = jnp.mean(hidden * hidden, axis=0, keepdims=True)
    out[...] = (hidden * lax.rsqrt(mean_square + 1e-05)).astype(out.dtype)

    for q in range(chunks):
        for offset in range(1, groups):
            for r in range(per):
                gather(q, offset, r).wait_send()

        @pl.loop(0, chips)
        def _(zt):
            mate_copy(q, zt).wait_send()

            @pl.when(zt != z)
            def _():
                up_copy(q, zt).wait_send()


def shards(node_feats, tile_vals, tile_rows, tile_cols, tile_count, degree, w_self, w_neigh):
    loop, groups = lax.axis_size("loop"), lax.axis_size("grp")
    chips = loop // 2
    features, nodes = node_feats.shape
    outputs = w_self.shape[1]
    slots, edge = tile_vals.shape[2], tile_vals.shape[3]
    per = nodes // edge
    chunks = CHUNKS
    part = features // chunks
    piece = (chips, chunks, part, nodes)
    dma = pltpu.SemaphoreType.DMA
    anywhere = pl.BlockSpec(memory_space=pl.ANY)
    scalars = pl.BlockSpec(memory_space=pltpu.SMEM)
    vector = pl.BlockSpec(memory_space=pltpu.VMEM)
    return pl.pallas_call(
        functools.partial(kernel, chips, groups, chunks),
        out_shape=jax.ShapeDtypeStruct((outputs, nodes), jnp.bfloat16),
        in_specs=[anywhere] * 4 + [scalars] * 3 + [vector],
        out_specs=vector,
        scratch_shapes=[pltpu.VMEM((groups * per, part, edge), jnp.bfloat16)] * chunks
        + [
            pltpu.VMEM((loop, slots, edge, edge), jnp.bfloat16),
            pltpu.VMEM(w_self.shape, jnp.bfloat16),
            pltpu.VMEM(w_neigh.shape, jnp.bfloat16),
            pltpu.VMEM((outputs, features), jnp.bfloat16),
            pltpu.VMEM((outputs, nodes), jnp.float32),
            pltpu.VMEM(piece, jnp.float32),
            pltpu.VMEM(piece, jnp.float32),
            pltpu.VMEM(piece, jnp.float32),
            pltpu.VMEM(piece, jnp.bfloat16),
            pltpu.VMEM(piece, jnp.bfloat16),
            pltpu.VMEM(piece, jnp.bfloat16),
            dma((3,)),
            dma((chunks, per)),
            dma((chunks, groups - 1, per)),
            dma((chunks, groups - 1, per)),
            dma((chips, chunks)),
            dma((chips, chunks)),
            dma((chips, chunks)),
            dma((chips, chunks)),
            dma((chips, chunks)),
        ],
        compiler_params=pltpu.CompilerParams(
            collective_id=0, has_side_effects=True, vmem_limit_bytes=60 * 2**20
        ),
    )(
        node_feats,
        tile_vals.reshape(tile_vals.shape[1:]),
        w_self,
        w_neigh,
        tile_rows.reshape(tile_rows.shape[1:]),
        tile_cols.reshape(tile_cols.shape[1:]),
        tile_count,
        degree.reshape(1, -1),
    )


def solution(mesh):
    return jax.shard_map(
        shards,
        mesh=mesh,
        in_specs=(
            P(None, ("loop", "grp")),
            P("loop", None, None, None, None),
            P("loop", None, None),
            P("loop", None, None),
            P("loop", None),
            P("loop"),
            P(),
            P(),
        ),
        out_specs=P(None, ("loop", "grp")),
        check_vma=False,
    )
```

time: 98.3 us -> 64.6 us (0.66)
  Pallas kernels: 0 us -> 62.7 us
  starting transfers between devices: 32.9 us -> 0 us
  matrix products: 21.9 us -> 0 us
  waiting for transfers between devices: 20.9 us -> 0 us
  local copies, waits for them, and re-layouts: 12.9 us -> 1.67 us
  other arithmetic: 8.25 us -> 0 us
    pallas_call x0 -> x1, Pallas kernels: none -> 62.7 us  [shards(): pl.pallas_call(functools.partial(kernel, chips, groups, chunks), out_shap...]
    ppermute x7 -> x0, starting transfers between devices: 24.2 us -> none  [from_behind(): lax.ppermute(shard, axis, [(i, (i + by) % size) for i in range(size)])]
    dot_general x26 -> x0, matrix products: 21.9 us -> none  [the longest x8 10.6 us: tile_terms(): jnp.einsum('kfc,krc->kfr', chosen, tiles, preferred_element_type=jnp.floa...]
    ppermute x7 -> x0, waiting for transfers between devices: 13.9 us -> none  [from_behind(): lax.ppermute(shard, axis, [(i, (i + by) % size) for i in range(size)])]
    all_to_all x2 -> x0, starting transfers between devices: 8.7 us -> none  [the longest x1 5.29 us: shards(): lax.all_to_all(node_feats, 'grp', split_axis=0, concat_axis=1, tiled=True)]
    all_to_all x2 -> x0, waiting for transfers between devices: 7.01 us -> none  [the longest x1 4.98 us: shards(): lax.all_to_all(neighbor, 'grp', split_axis=1, concat_axis=0, tiled=True)]
    dynamic_slice x8 -> x0, local copies, waits for them, and re-layouts: 5.85 us -> none  [contribution(): lax.dynamic_index_in_dim(own_counts, target, 0, False)]
    eq x8 -> x0, local copies, waits for them, and re-layouts: 5.67 us -> none  [tile_terms(): picker = (col_ids[:, None] == block_ids[None, :]).astype(jnp.bfloat16)]
  transfers between devices with their start and end apart: 9 -> 0, of which waited for: 9 -> 0; matrix products, arithmetic and copies ran while one was open for 37% -> 0% of each run, Pallas kernels for 0% -> 0%
where the time goes in v1:
time: 64.6 us; the launch traced here: 64.4 us
  Pallas kernels  62.7 us (97%)
  local copies, waits for them, and re-layouts  1.67 us (3%)
    pallas_call x1, Pallas kernels, shards(): pl.pallas_call(functools.partial(kernel, chips, groups, chunks), out_shap...  62.7 us
    unnamed x1, local copies, waits for them, and re-layouts  1.67 us

profile of v1, /device:TPU:0, one launch (start us, length us, event | category | flops | bytes accessed | tf_op | source)
XLA Modules:
  0.0 64.4 jit_solution(4260429074690877059)
XLA Ops:
  0.0 62.7 %shard_map.82 = bf16[512,256]{1,0:T(8,128)(2,1)} custom-call(bf16[512,256]{1,0:T(8,128)(2,1)} %feats.1, bf16[8,10,128,128]{3,2,1,0:T(8,128)(2,1)} %bitcast.4, bf16[512,512]{1,0:T(8,128)(2,1)} %w_self_hbm.1, bf16[512,512]{1,0:T(8,128)(2,1)} %w_neigh_hbm.1, s32[8,10]{1,0:T(8,128)} %bitcast.5, s32[8,10]{1,0:T(8,128)} %bitcast.6, s32[1,8]{1,0:T(1,128)} %counts.1, ...), custom_call_target="tpu_custom_call" | custom-call | tf_op jit(solution)/shard_map/pallas_call | solution.py:284
  62.7 1.7 %copy.10 = bf16[512,256]{1,0:T(8,128)(2,1)} copy(bf16[512,256]{1,0:T(8,128)(2,1)} %shard_map.82) | data formatting | bytes 524288

commit v2 on v1

--- a/solution.py
+++ b/solution.py
@@ -8,7 +8,7 @@
 from jax.sharding import PartitionSpec as P
 
 MESH = pl.DeviceIdType.MESH
-CHUNKS = 4
+CHUNKS = 2
 
 
 def kernel(
@@ -114,10 +114,12 @@
     inner = jnp.where((z > 0) & (z < chips - 1), 1, 0)
     pl.semaphore_wait(barrier, groups + 1 + inner)
 
-    for q in range(chunks):
+    def gather_start(q):
         for offset in range(1, groups):
             for r in range(per):
                 gather(q, offset, r).start()
+
+    gather_start(0)
 
     def masked(t, k):
         tile = tiles[t, k]
@@ -147,6 +149,7 @@
         return total
 
     upward = 2 * z < chips
+    outer = (z == 0) | (z == chips - 1)
 
     def target_at(i):
         return jnp.where(upward, chips - 1 - i, i)
@@ -160,6 +163,8 @@
         for offset in range(1, groups):
             for r in range(per):
                 gather(q, offset, r).wait_recv()
+        if q + 1 < chunks:
+            gather_start(q + 1)
         if q == 0:
             for r in range(per):
                 own_copy(q, r).wait()
@@ -178,37 +183,44 @@
             mine = mine + mate_in[zt, q]
             own[zt, q] = mine
 
-            @pl.when((z == 0) & (zt > 0))
+            @pl.when(outer & (i < chips - 1))
             def _():
                 chain_out[zt, q] = mine.astype(chain_out.dtype)
-                up_copy(q, zt).start()
-
-            @pl.when((z == chips - 1) & (zt < chips - 1))
-            def _():
-                chain_out[zt, q] = mine.astype(chain_out.dtype)
-                down_copy(q, zt).start()
-
-    def relay(q):
+
+                @pl.when(z == 0)
+                def _():
+                    up_copy(q, zt).start()
+
+                @pl.when(z > 0)
+                def _():
+                    down_copy(q, zt).start()
+
+    def relay(stage):
+        up_q, down_q = stage + 1 - z, stage + 2 + z - chips
+        up_live = (z > 0) & (up_q >= 0) & (up_q < chunks)
+        down_live = (z < chips - 1) & (down_q >= 0) & (down_q < chunks)
+
         @pl.loop(0, chips - 1)
         def _(d):
             high = chips - 1 - d
 
-            @pl.when((z > 0) & (high > z))
-            def _():
-                up_copy(q, high).wait_recv()
-                chain_out[high, q] = (
-                    own[high, q] + from_low[high, q].astype(jnp.float32)
+            @pl.when(up_live & (high > z))
+            def _():
+                up_copy(up_q, high).wait_recv()
+                chain_out[high, up_q] = (
+                    own[high, up_q] + from_low[high, up_q].astype(jnp.float32)
                 ).astype(chain_out.dtype)
-                up_copy(q, high).start()
-
-            @pl.when((z < chips - 1) & (d < z))
-            def _():
-                down_copy(q, d).wait_recv()
-                chain_out[d, q] = (
-                    own[d, q] + from_high[d, q].astype(jnp.float32)
+                up_copy(up_q, high).start()
+
+            @pl.when(down_live & (d < z))
+            def _():
+                down_copy(down_q, d).wait_recv()
+                chain_out[d, down_q] = (
+                    own[d, down_q] + from_high[d, down_q].astype(jnp.float32)
                 ).astype(chain_out.dtype)
-                down_copy(q, d).start()
-
+                down_copy(down_q, d).start()
+
+    def finish(q):
         @pl.when(z > 0)
         def _():
             up_copy(q, z).wait_recv()
@@ -245,9 +257,11 @@
                 )
                 total = term if total is None else total + term
             pre[...] = total
-        else:
-            relay(q - 1)
-    relay(chunks - 1)
+        relay(q)
+    for stage in range(chunks, chunks + max(chips - 3, 0)):
+        relay(stage)
+    for q in range(chunks):
+        finish(q)
 
     hidden = jnp.maximum(pre[...], 0.0)
     mean_square = jnp.mean(hidden * hidden, axis=0, keepdims=True)

time: 64.6 us -> 41.1 us (0.64)
  Pallas kernels: 62.7 us -> 39.3 us
    pallas_call x1, Pallas kernels: 62.7 us -> 39.3 us  [shards(): pl.pallas_call(functools.partial(kernel, chips, groups, chunks), out_shap...]
where the time goes in v2:
time: 41.1 us; the launch traced here: 40.9 us
  Pallas kernels  39.3 us (96%)
  local copies, waits for them, and re-layouts  1.67 us (4%)
    pallas_call x1, Pallas kernels, shards(): pl.pallas_call(functools.partial(kernel, chips, groups, chunks), out_shap...  39.3 us
    unnamed x1, local copies, waits for them, and re-layouts  1.67 us

profile of v2, /device:TPU:0, one launch (start us, length us, event | category | flops | bytes accessed | tf_op | source)
XLA Modules:
  0.0 40.9 jit_solution(16501447511714217009)
XLA Ops:
  0.0 39.3 %shard_map.82 = bf16[512,256]{1,0:T(8,128)(2,1)} custom-call(bf16[512,256]{1,0:T(8,128)(2,1)} %feats.1, bf16[8,10,128,128]{3,2,1,0:T(8,128)(2,1)} %bitcast.4, bf16[512,512]{1,0:T(8,128)(2,1)} %w_self_hbm.1, bf16[512,512]{1,0:T(8,128)(2,1)} %w_neigh_hbm.1, s32[8,10]{1,0:T(8,128)} %bitcast.5, s32[8,10]{1,0:T(8,128)} %bitcast.6, s32[1,8]{1,0:T(1,128)} %counts.1, ...), custom_call_target="tpu_custom_call" | custom-call | tf_op jit(solution)/shard_map/pallas_call | solution.py:298
  39.3 1.7 %copy.10 = bf16[512,256]{1,0:T(8,128)(2,1)} copy(bf16[512,256]{1,0:T(8,128)(2,1)} %shard_map.82) | data formatting | bytes 524288
